TPU v7x, 32 devices: a whole 2x2x4 slice. The times are simulated.
32 devices in a mesh: tm: 8 (over z, x), chan: 4 (over y, core).
Axes of the slice: x: 2, y: 2, z: 4, core: 2. Of those that a mesh axis runs over, the one named last changes fastest.
Arguments:
- features: bfloat16 [49152, 512], P('tm', 'chan'), may hold values from -6 to 6
- snake_alpha: float32 [512], P('chan'), may hold values from 0.5 to 3
- down_weight: bfloat16 [512, 16, 1024], P(None, None, 'chan'), may hold values from -0.0625 to 0.0625
- grad_out: bfloat16 [6144, 1024], P('tm', 'chan'), may hold values from -6 to 6
Outputs:
- encoded: bfloat16 [6144, 1024], P('tm', 'chan')
- grad_features: bfloat16 [49152, 512], P('tm', 'chan')
- grad_down: bfloat16 [1024, 16, 512], P('tm', None, 'chan')
All inputs are finite; a program needn't handle non-finite values.
Results may differ from a plain program's by a relative error of at most 0.0049.
Values may be sent and summed in bfloat16 or wider, within the bound.
A program may use at most 128 MiB of HBM per device.

v0:
```python
import math

import jax
import jax.numpy as jnp
from jax import lax
from jax.sharding import PartitionSpec as P

STRIDE = 8


def with_halo(block, sides, width):
    for axis, dim in sides:
        count = lax.axis_size(axis)
        forward = [(i, i + 1) for i in range(count - 1)]
        backward = [(target, source) for source, target in forward]
        low = lax.ppermute(
            lax.slice_in_dim(block, block.shape[dim] - width, None, axis=dim), axis, forward
        )
        high = lax.ppermute(lax.slice_in_dim(block, 0, width, axis=dim), axis, backward)
        block = jnp.concatenate([low, block, high], axis=dim)
    return block


def snake(values, alpha):
    return values + jnp.sin(alpha * values) ** 2 / alpha


def shards(features, snake_alpha, down_weight, grad_out):
    frames = features.shape[0]
    local_chans = features.shape[1]
    blocks_out = frames // STRIDE
    offset = STRIDE // 2
    wide = features.astype(jnp.float32)
    snaked = snake(wide, snake_alpha).astype(jnp.bfloat16)
    padded = with_halo(snaked, (("tm", 0),), offset)
    local_tiled = padded.reshape(blocks_out + 1, STRIDE, local_chans)
    full_cols = lax.all_gather(padded, "chan", axis=1, tiled=True)
    tiled = full_cols.reshape(blocks_out + 1, STRIDE, full_cols.shape[1])
    encoded = (
        jnp.einsum(
            "ujr,rjp->up", tiled[:-1], down_weight[:, :STRIDE], preferred_element_type=jnp.float32
        )
        + jnp.einsum(
            "ujr,rjp->up", tiled[1:], down_weight[:, STRIDE:], preferred_element_type=jnp.float32
        )
    ).astype(jnp.bfloat16)
    grad_pad = with_halo(grad_out, (("tm", 0),), 1)
    grad_full = lax.all_gather(grad_pad, "chan", axis=1, tiled=True)
    spread = jnp.einsum(
        "up,rjp->ujr", grad_pad[1:], down_weight[:, :STRIDE], preferred_element_type=jnp.float32
    ) + jnp.einsum(
        "up,rjp->ujr", grad_pad[:-1], down_weight[:, STRIDE:], preferred_element_type=jnp.float32
    )
    partial_terms = spread.reshape(frames + STRIDE, down_weight.shape[0])[offset : offset + frames]
    grad_snaked = lax.psum_scatter(partial_terms, "chan", scatter_dimension=1, tiled=True)
    grad_features = (grad_snaked * (1.0 + jnp.sin(2.0 * snake_alpha * wide))).astype(jnp.bfloat16)
    grad_inner = grad_full[1:-1]
    scale = 1.0 / math.sqrt(blocks_out * lax.axis_size("tm"))
    lower = jnp.einsum(
        "ujr,up->pjr", local_tiled[:-1], grad_inner, preferred_element_type=jnp.float32
    )
    upper = jnp.einsum(
        "ujr,up->pjr", local_tiled[1:], grad_inner, preferred_element_type=jnp.float32
    )
    summed = lax.psum_scatter(
        jnp.concatenate([lower, upper], axis=1), "tm", scatter_dimension=0, tiled=True
    )
    grad_down = (summed * scale).astype(jnp.bfloat16)
    return (encoded, grad_features, grad_down)


def solution(mesh):
    placed = (P("tm", "chan"), P("chan"), P(None, None, "chan"), P("tm", "chan"))
    return jax.shard_map(
        shards,
        mesh=mesh,
        in_specs=placed,
        out_specs=(P("tm", "chan"), P("tm", "chan"), P("tm", None, "chan")),
        check_vma=False,
    )
```

profile of v0, /device:TPU:0, one launch (start us, length us, event | category | flops | bytes accessed | tf_op | source)
XLA Modules:
  0.0 404.4 jit_solution(10917598290743750689)
XLA Ops:
  7.9 4.8 %collective-permute-start.3 = (bf16[1,256]{1,0:T(2,128)(2,1)S(1)}, bf16[1,256]{1,0:T(2,128)(2,1)S(1)}, u32[]{:S(2)}, u32[]{:S(2)}) collective-permute-start(bf16[1,256]{1,0:T(2,128)(2,1)S(1)} %get-tuple-element.20), channel_id=1, source_target_pairs={{0,4},{4,8},{8,12},{12,16},{16,20},{20,24},{24,28},{1,5},{5,9},{9,... | collective-permute-start | bytes 1544 | tf_op jit(solution)/shard_map/ppermute | solution.py:16
  12.8 1.4 collective-permute-start.2
  14.2 2.5 fusion.49
  16.7 1.9 fusion.12
  18.7 6.7 %add_bitcast_fusion = f32[769,8,512]{2,0,1:T(8,128)} fusion(f32[769,512,8]{1,0,2:T(8,128)S(1)} %fusion.12, bf16[512,8,256]{2,1,0:T(8,128)(2,1)S(1)} %get-tuple-element.11, bf16[1,256]{1,0:T(2,128)(2,1)S(1)} %collective-permute-done.2, bf16[768,256]{1,0:T(8,128)(2,1)S(1)} %copy-done.4), kind=kOutput, calls=%fused_computation | convolution fusion | flops 1616647168 | bytes 27689472 | tf_op jit(solution)/shard_map/up,rjp->ujr/dot_general | solution.py:49
  25.4 16.4 %copy.59 = f32[769,8,512]{2,1,0:T(8,128)} copy(f32[769,8,512]{2,0,1:T(8,128)} %add_bitcast_fusion) | data formatting | bytes 25198592 | tf_op jit(solution)/shard_map/add | solution.py:49
  41.9 10.9 %slice.76 = f32[6144,512]{1,0:T(8,128)} slice(f32[6152,512]{1,0:T(8,128)} %bitcast.31), slice={[4:6148], [0:512]} | slice | bytes 25165824 | tf_op jit(solution)/shard_map/slice | solution.py:54
  54.4 100.0 %reduce-scatter.3.cloned.1.call-done = f32[6144,128]{1,0:T(8,128)} async-done(((f32[6144,512]{1,0:T(8,128)}), f32[6144,128]{1,0:T(8,128)}) %reduce-scatter.3.cloned.1.call-update) | async-done | bytes 3145744 | tf_op jit(solution)/shard_map/reduce_scatter | solution.py:55
  154.4 23.1 %fusion.11 = (bf16[6144,128]{1,0:T(8,128)(2,1)}, bf16[6144,128]{1,0:T(8,128)(2,1)S(1)}) fusion(f32[6144,128]{1,0:T(8,128)} %reduce-scatter.3.cloned.1.call-done, bf16[6144,128]{1,0:T(8,128)(2,1)S(1)} %copy-done.5, f32[128]{0:T(128)S(1)} %broadcast_multiply_fusion, f32[128]{0:T(128)S(1)} %copy-done.6), kind=kLoop, calls=%fused_computation.19 | loop fusion | flops 7864320 | bytes 7865344 | tf_op jit(solution)/shard_map/convert_element_type | solution.py:56
  177.5 3.4 collective-permute-start
  180.9 1.3 collective-permute-start.1
  182.2 4.2 %collective-permute-done.1 = bf16[4,128]{1,0:T(4,128)(2,1)S(1)} collective-permute-done((bf16[4,128]{1,0:T(4,128)(2,1)S(1)}, bf16[4,128]{1,0:T(4,128)(2,1)S(1)}, u32[]{:S(2)}, u32[]{:S(2)}) %collective-permute-start.1) | collective-permute-done | bytes 1056 | tf_op jit(solution)/shard_map/ppermute | solution.py:19
  186.3 8.7 %concatenate.21 = bf16[6152,128]{1,0:T(8,128)(2,1)} concatenate(bf16[4,128]{1,0:T(4,128)(2,1)S(1)} %collective-permute-done, bf16[6144,128]{1,0:T(8,128)(2,1)S(1)} %get-tuple-element.16, bf16[4,128]{1,0:T(4,128)(2,1)S(1)} %collective-permute-done.1), dimensions={0} | concatenate | bytes 3149824 | tf_op jit(solution)/shard_map/concatenate | solution.py:20
  195.1 1.6 fusion.18
  196.7 3.9 fusion.21
  200.6 1.8 fusion.19
  202.5 4.2 %pad_maximum_fusion = f32[1024,16,128]{2,0,1:T(8,128)} fusion(f32[1024,8,128]{2,0,1:T(8,128)S(1)} %fusion.19, f32[1024,8,128]{2,0,1:T(8,128)S(1)} %fusion.21), kind=kLoop, calls=%fused_computation.2 | loop fusion | flops 2097152 | bytes 16777216 | tf_op jit(solution)/shard_map/concatenate | solution.py:66
  206.8 35.7 %all-gather.3.cloned.1.call-done = bf16[6152,512]{1,0:T(8,128)(2,1)} async-done(((bf16[6152,128]{1,0:T(8,128)(2,1)}), bf16[6152,512]{1,0:T(8,128)(2,1)}) %all-gather.3.cloned.1.call-update) | async-done | bytes 6299664 | tf_op jit(solution)/shard_map/all_gather | solution.py:37
  242.5 5.3 %slice_bitcast_fusion.1 = (bf16[768,8,512]{2,1,0:T(8,128)(2,1)S(1)}, bf16[768,8,512]{2,1,0:T(8,128)(2,1)S(1)}) fusion(bf16[6152,512]{1,0:T(8,128)(2,1)} %all-gather.3.cloned.1.call-done), kind=kLoop, calls=%fused_computation.4 | loop fusion | bytes 25165824 | tf_op jit(solution)/shard_map/slice | solution.py:41
  247.8 3.9 fusion.28
  251.7 4.7 %fusion.38 = bf16[768,256]{1,0:T(8,128)(2,1)} fusion(f32[768,256]{1,0:T(8,128)S(1)} %fusion.28, bf16[512,8,256]{2,1,0:T(8,128)(2,1)S(1)} %copy-done.3, bf16[768,8,512]{2,1,0:T(8,128)(2,1)S(1)} %get-tuple-element.9), kind=kOutput, calls=%fused_computation.37 | convolution fusion | flops 1611005952 | bytes 9568256 | tf_op jit(solution)/shard_map/ujr,rjp->up/dot_general | solution.py:40
  256.4 138.9 %reduce-scatter.5.cloned.1.call-done = f32[128,16,128]{2,0,1:T(8,128)} async-done(((f32[1024,16,128]{2,0,1:T(8,128)}), f32[128,16,128]{2,0,1:T(8,128)}) %reduce-scatter.5.cloned.1.call-update) | async-done | bytes 1048592 | tf_op jit(solution)/shard_map/reduce_scatter | solution.py:65
  395.4 1.4 multiply_convert_fusion
  396.7 1.1 copy.23
  (35 shorter events, 2.5 us)
Async XLA Ops:
  7.2 147.3 %reduce-scatter.3.cloned.1.call-start = ((), (), s32[]{:S(2)}) async-start(), calls=%async_computation.3 | async-start | bytes 15728640 | tf_op jit(solution)/shard_map/reduce_scatter | solution.py:55
  7.9 8.8 %collective-permute-start.3 = (bf16[1,256]{1,0:T(2,128)(2,1)S(1)}, bf16[1,256]{1,0:T(2,128)(2,1)S(1)}, u32[]{:S(2)}, u32[]{:S(2)}) collective-permute-start(bf16[1,256]{1,0:T(2,128)(2,1)S(1)} %get-tuple-element.20), channel_id=1, source_target_pairs={{0,4},{4,8},{8,12},{12,16},{16,20},{20,24},{24,28},{1,5},{5,9},{9,... | collective-permute-start | bytes 1544 | tf_op jit(solution)/shard_map/ppermute | solution.py:16
  12.8 4.0 copy-start.4
  12.8 5.9 %collective-permute-start.2 = (bf16[1,256]{1,0:T(2,128)(2,1)S(1)}, bf16[1,256]{1,0:T(2,128)(2,1)S(1)}, u32[]{:S(2)}, u32[]{:S(2)}) collective-permute-start(bf16[1,256]{1,0:T(2,128)(2,1)S(1)} %get-tuple-element.19), channel_id=1, source_target_pairs={{4,0},{8,4},{12,8},{16,12},{20,16},{24,20},{28,24},{5,1},{9,5},{13... | collective-permute-start | bytes 1544 | tf_op jit(solution)/shard_map/ppermute | solution.py:19
  16.7 1.9 copy-start
  16.7 2.0 copy-start.2
  52.7 1.6 copy-start.6
  52.8 101.7 %copy-start.5 = (bf16[6144,128]{1,0:T(8,128)(2,1)S(1)}, bf16[6144,128]{1,0:T(8,128)(2,1)}, u32[]{:S(2)}) copy-start(bf16[6144,128]{1,0:T(8,128)(2,1)} %param.4) | copy-start | bytes 4718596
  52.8 143.9 %all-gather.5.cloned.1.call-start = ((), (), s32[]{:S(2)}) async-start(), calls=%async_computation.4 | async-start | bytes 2293760 | tf_op jit(solution)/shard_map/all_gather | solution.py:48
  54.3 188.2 %all-gather.3.cloned.1.call-start = ((), (), s32[]{:S(2)}) async-start(), calls=%async_computation.2 | async-start | bytes 7874560 | tf_op jit(solution)/shard_map/all_gather | solution.py:37
  177.5 4.7 %collective-permute-start = (bf16[4,128]{1,0:T(4,128)(2,1)S(1)}, bf16[4,128]{1,0:T(4,128)(2,1)S(1)}, u32[]{:S(2)}, u32[]{:S(2)}) collective-permute-start(bf16[4,128]{1,0:T(4,128)(2,1)S(1)} %get-tuple-element.18), channel_id=1, source_target_pairs={{0,4},{4,8},{8,12},{12,16},{16,20},{20,24},{24,28},{1,5},{5,9},{9,... | collective-permute-start | bytes 3080 | tf_op jit(solution)/shard_map/ppermute | solution.py:16
  180.9 5.5 %collective-permute-start.1 = (bf16[4,128]{1,0:T(4,128)(2,1)S(1)}, bf16[4,128]{1,0:T(4,128)(2,1)S(1)}, u32[]{:S(2)}, u32[]{:S(2)}) collective-permute-start(bf16[4,128]{1,0:T(4,128)(2,1)S(1)} %get-tuple-element.17), channel_id=1, source_target_pairs={{4,0},{8,4},{12,8},{16,12},{20,16},{24,20},{28,24},{5,1},{9,5},{13... | collective-permute-start | bytes 3080 | tf_op jit(solution)/shard_map/ppermute | solution.py:19
  195.1 200.3 %reduce-scatter.5.cloned.1.call-start = ((), (), s32[]{:S(2)}) async-start(), calls=%async_computation.5 | async-start | bytes 9437184 | tf_op jit(solution)/shard_map/reduce_scatter | solution.py:65
  196.7 3.9 copy-start.7
  206.7 41.0 %copy-start.1 = (bf16[512,8,256]{2,1,0:T(8,128)(2,1)S(1)}, bf16[512,8,256]{2,1,0:T(8,128)(2,1)}, u32[]{:S(2)}) copy-start(bf16[512,8,256]{2,1,0:T(8,128)(2,1)} %copy-done) | copy-start | bytes 6291460
  247.8 3.9 copy-start.3
Sparse Core Ops, SparseCore 0:
  52.9 101.4 reduce-scatter.2
  156.6 21.1 all-gather.4
  195.2 47.2 all-gather.2
  246.0 149.3 reduce-scatter.4
where the time goes:
time: 405 us; the launch traced here: 404 us
  waiting for transfers between devices  279 us (69%)
  local copies, waits for them, and re-layouts  46.2 us (11%)
  other arithmetic  31.2 us (8%)
  matrix products  23 us (6%)
  between operations  14 us (3%)
  starting transfers between devices  11.1 us (3%)
    reduce_scatter x1, waiting for transfers between devices, shards(): lax.psum_scatter(jnp.concatenate([lower, upper], axis=1), 'tm', scatter_d...  139 us
    reduce_scatter x1, waiting for transfers between devices, shards(): lax.psum_scatter(partial_terms, 'chan', scatter_dimension=1, tiled=True)  100 us
    all_gather x1, waiting for transfers between devices, shards(): full_cols = lax.all_gather(padded, 'chan', axis=1, tiled=True)  35.7 us
    convert_element_type x1, other arithmetic, shards(): (grad_snaked * (1.0 + jnp.sin(2.0 * snake_alpha * wide))).astype(jnp.bflo...  23.1 us
    add x1, local copies, waits for them, and re-layouts, shards(): jnp.einsum('up,rjp->ujr', grad_pad[1:], down_weight[:, :STRIDE], preferre...  16.4 us
    slice x1, local copies, waits for them, and re-layouts, shards(): spread.reshape(frames + STRIDE, down_weight.shape[0])  10.9 us
    concatenate x1, local copies, waits for them, and re-layouts, with_halo(): block = jnp.concatenate([low, block, high], axis=dim)  8.69 us
    ppermute x2, starting transfers between devices, with_halo(): lax.ppermute(lax.slice_in_dim(block, block.shape[dim] - width, None, axis...  8.2 us
  transfers between devices with their start and end apart: 8, of which 4 were waited for; matrix products, arithmetic and copies ran while one was open for 16% of the time, Pallas kernels for 0%

commit v1 on v0

v1 whole, which is shorter than its diff:
```python
import functools
import math

import jax
import jax.numpy as jnp
from jax import lax
from jax.experimental import pallas as pl
from jax.experimental.pallas import tpu as pltpu
from jax.sharding import PartitionSpec as P

STRIDE = 8
TAPS = 16
HALO = 16
PARTS = 4
BF = jnp.bfloat16
F32 = jnp.float32

PI_HIGH = 3.140625
PI_LOW = math.pi - PI_HIGH


def bit_reversed(value, bits):
    out = 0
    for _ in range(bits):
        out = out * 2 + value % 2
        value //= 2
    return out


def sin_cos(angle):
    turns = jnp.floor(angle * (1.0 / math.pi) + 0.5)
    r = (angle - turns * PI_HIGH) - turns * PI_LOW
    q = r * r
    s = -1.0 / math.factorial(11)
    for n, sign in ((9, 1.0), (7, -1.0), (5, 1.0), (3, -1.0), (1, 1.0)):
        s = s * q + sign / math.factorial(n)
    c = 1.0 / math.factorial(12)
    for n, sign in ((10, -1.0), (8, 1.0), (6, -1.0), (4, 1.0), (2, -1.0), (0, 1.0)):
        c = c * q + sign / math.factorial(n)
    return s * r, c


def dot(a, b, dims):
    return lax.dot_general(a, b, (dims, ((), ())), preferred_element_type=F32)


def kernel(
    count, feat, alpha, weight, grad, enc_out, gf_out, gd_out,
    snaked, factor, cols, gfull, gturn, gprev, gnext, gwide,
    wstage, wsend, wbuf, acc, sends, recvs, esum, esend, erecv, ysend, yrecv,
    flow, fhigh, glow, ghigh, gdwide,
    fsem, gsem, wsem, hsem, rsem, esem,
):
    bits = count.bit_length() - 1
    frames, ci = feat.shape
    units, pb = grad.shape
    width = TAPS * ci
    chunk = width // PARTS
    outs = 4 * pb
    rows = outs // count
    t = lax.axis_index("tm")
    ch = lax.axis_index("chan")
    nxt = lax.rem(t + 1, count)
    prv = lax.rem(t + count - 1, count)

    def flip(value, bit):
        return value + bit - 2 * bit * (lax.rem(value // bit, 2))

    sib = flip(ch, 1)
    par = flip(ch, 2)
    opp = flip(sib, 2)
    peers = (None, sib, par, opp)

    def remote(src, dst, sems, i, **where):
        return pltpu.make_async_remote_copy(
            src_ref=src, dst_ref=dst, send_sem=sems.at[0, i], recv_sem=sems.at[1, i],
            device_id=where, device_id_type=pl.DeviceIdType.MESH,
        )

    barrier = pltpu.get_barrier_semaphore()
    greet = [dict(chan=sib), dict(chan=par), dict(chan=opp), dict(tm=nxt), dict(tm=prv)]
    greet += [dict(tm=flip(t, 1 << s)) for s in range(bits)]
    for where in greet:
        pl.semaphore_signal(barrier, inc=1, device_id=where, device_id_type=pl.DeviceIdType.MESH)
    pl.semaphore_wait(barrier, len(greet))

    g_par = remote(grad, gfull.at[ch], gsem, 0, chan=par)
    g_sib = remote(grad, gfull.at[ch], gsem, 1, chan=sib)
    g_fwd = remote(gfull.at[par], gfull.at[par], gsem, 2, chan=sib)
    f_up = remote(feat.at[pl.ds(frames - HALO, HALO)], flow, fsem, 0, tm=nxt)
    f_down = remote(feat.at[pl.ds(0, HALO)], fhigh, fsem, 1, tm=prv)
    g_par.start()
    g_sib.start()
    f_up.start()
    f_down.start()

    def turn(owner, dst):
        for half in range(pb // 128):
            lanes = pl.ds(half * 128, 128)
            wstage[...] = weight[pl.ds(owner * ci, ci), :, lanes].astype(F32).reshape(ci * TAPS, 128)
            for k in range(TAPS):
                dst[pl.ds(k * ci, ci), lanes] = wstage[pl.ds(k, ci, stride=TAPS), :].astype(BF)

    w_copies = {}
    for r in (2, 3, 1):
        turn(peers[r], wsend.at[r - 1])
        w_copies[r] = remote(wsend.at[r - 1], wbuf.at[ch], wsem, r - 1, chan=peers[r])
        w_copies[r].start()
    turn(ch, wbuf.at[ch])
    gfull[ch] = grad[...]

    a = alpha[...]
    inv = 1.0 / a

    def activate(x):
        wide = x.astype(F32)
        s, c = sin_cos(a * wide)
        return wide + s * s * inv, 1.0 + 2.0 * (s * c)

    step = 256

    def snake_step(i, _):
        at = pl.multiple_of(i * step, step)
        val, fac = activate(feat[pl.ds(at, step), :])
        snaked[pl.ds(pl.multiple_of(HALO + at, HALO), step), :] = val
        factor[pl.ds(at, step), :] = fac
        return 0

    lax.fori_loop(0, frames // step, snake_step, 0)

    g_par.wait_recv()
    g_fwd.start()

    f_up.wait_recv()
    f_down.wait_recv()
    low_on = jnp.where(t > 0, 1.0, 0.0)
    high_on = jnp.where(t < count - 1, 1.0, 0.0)
    snaked[pl.ds(0, HALO), :] = activate(flow[...])[0] * low_on
    snaked[pl.ds(HALO + frames, HALO), :] = activate(fhigh[...])[0] * high_on
    for k in range(TAPS):
        cols[:, pl.ds(k * ci, ci)] = snaked[
            pl.ds(HALO - STRIDE // 2 + k, units, stride=STRIDE), :
        ].astype(BF)

    g_sib.wait_recv()
    g_fwd.wait_recv()
    h_up = remote(gfull.at[:, pl.ds(units - HALO, HALO), :], glow, hsem, 0, tm=nxt)
    h_down = remote(gfull.at[:, pl.ds(0, HALO), :], ghigh, hsem, 1, tm=prv)
    h_up.start()
    h_down.start()

    for blk in range(4):
        for part in range(pb // 128):
            turned = gfull[blk, :, pl.ds(part * 128, 128)].astype(F32).T.astype(BF)
            first = blk * pb + part * 128
            size = min(rows, 128)
            for j in range(128 // size):
                p = first + j * size
                d, rest = p // rows, p % rows
                gturn[pl.ds(bit_reversed(d, bits) * rows + rest, size), :] = turned[
                    j * size : (j + 1) * size, :
                ]

    bit_of = [lax.rem(t // (1 << s), 2) for s in range(bits)]
    half = outs // 2
    other = pl.multiple_of((1 - bit_of[0]) * half, half)
    mine = pl.multiple_of(bit_of[0] * half, half)

    def stage(s, c):
        return remote(
            sends[s].at[c], recvs[s].at[c], rsem, s * PARTS + c, tm=flip(t, 1 << s)
        )

    def first_half(c, _):
        lanes = pl.ds(pl.multiple_of(c * chunk, chunk), chunk)
        sends[0][c] = dot(gturn[pl.ds(other, half), :], cols[:, lanes], ((1,), (0,))).astype(BF)
        stage(0, c).start()
        return 0

    lax.fori_loop(0, PARTS, first_half, 0)

    def second_half(c, _):
        lanes = pl.ds(pl.multiple_of(c * chunk, chunk), chunk)
        acc[c] = dot(gturn[pl.ds(mine, half), :], cols[:, lanes], ((1,), (0,)))
        return 0

    lax.fori_loop(0, PARTS, second_half, 0)

    scale = 1.0 / math.sqrt(units * count)

    base = [0]
    for s in range(1, bits):
        base.append(base[-1] + bit_of[s] * (half >> s))

    def advance(s, c):
        size = half >> s
        copy = stage(s, c)
        copy.wait_recv()
        if s + 1 < bits:
            nsize = size // 2
            keep = pl.multiple_of(base[s + 1], nsize)
            give = pl.multiple_of(base[s] + (1 - bit_of[s + 1]) * nsize, nsize)
            here = pl.multiple_of(bit_of[s + 1] * nsize, nsize)
            there = pl.multiple_of((1 - bit_of[s + 1]) * nsize, nsize)
            sends[s + 1][c] = (
                acc[c, pl.ds(give, nsize), :] + recvs[s][c, pl.ds(there, nsize), :].astype(F32)
            ).astype(BF)
            stage(s + 1, c).start()
            acc[c, pl.ds(keep, nsize), :] = acc[c, pl.ds(keep, nsize), :] + recvs[s][
                c, pl.ds(here, nsize), :
            ].astype(F32)
        else:
            held = pl.multiple_of(base[s], size)
            total = (acc[c, pl.ds(held, size), :] + recvs[s][c].astype(F32)) * scale
            taps = chunk // ci
            for j in range(taps):
                gdwide[pl.ds(c * taps + j, size, stride=TAPS), :] = total[:, j * ci : (j + 1) * ci]

    events = sorted(
        ((c + s * 1.3, s, c) for s in range(bits) for c in range(PARTS))
    )
    events = [(s, c) for _, s, c in events]

    def run(limit):
        while events and events[0][1] + events[0][0] <= limit:
            advance(*events.pop(0))

    run(2)

    h_up.wait_recv()
    h_down.wait_recv()

    def shifted(blk, _):
        gwide[pl.ds(0, HALO), :] = glow[blk].astype(F32) * low_on
        gwide[pl.ds(HALO, units), :] = gfull[blk].astype(F32)
        gwide[pl.ds(HALO + units, HALO), :] = ghigh[blk].astype(F32) * high_on
        gprev[blk] = gwide[pl.ds(HALO - 1, units), :].astype(BF)
        gnext[blk] = gwide[pl.ds(HALO + 1, units), :].astype(BF)
        return 0

    lax.fori_loop(0, 4, shifted, 0)

    for r in (1, 2, 3):
        w_copies[r].wait_recv()

    def encode(d, _):
        esum[d] = dot(cols[...], wbuf[d], ((1,), (0,)))
        return 0

    lax.fori_loop(0, 4, encode, 0)
    esend[0] = esum[sib].astype(BF)
    esend[1] = esum[opp].astype(BF)
    e_sib = remote(esend, erecv, esem, 0, chan=sib)
    e_par = remote(ysend, yrecv, esem, 1, chan=par)
    e_sib.start()

    run(3)

    e_sib.wait_recv()
    ysend[...] = (esum[par] + erecv[1].astype(F32)).astype(BF)
    e_par.start()

    quarter = 4 * ci
    tile = units // 3

    def spread(i, _):
        at = pl.multiple_of(i * tile, tile)
        us = pl.ds(at, tile)
        for lo, own, side, shift in ((0, 1, 3, gprev), (4, 2, 0, gnext)):
            total = jnp.zeros((tile, quarter), F32)
            for blk in range(4):
                total += dot(
                    gfull[blk, us, :], wbuf[blk, pl.ds(own * quarter, quarter), :], ((1,), (1,))
                )
                total += dot(
                    shift[blk, us, :], wbuf[blk, pl.ds(side * quarter, quarter), :], ((1,), (1,))
                )
            for j in range(4):
                snaked[pl.ds(at * STRIDE + lo + j, tile, stride=STRIDE), :] = total[
                    :, j * ci : (j + 1) * ci
                ]
        return 0

    lax.fori_loop(0, 3, spread, 0)

    def finish(i, _):
        at = pl.multiple_of(i * step, step)
        here = pl.ds(at, step)
        gf_out[here, :] = (snaked[here, :] * factor[here, :]).astype(BF)
        return 0

    lax.fori_loop(0, frames // step, finish, 0)

    e_par.wait_recv()
    enc_out[...] = (esum[ch] + erecv[0].astype(F32) + yrecv[...].astype(F32)).astype(BF)

    run(100)
    gd_out[...] = gdwide[...].reshape(rows, TAPS, ci).astype(BF)

    for copy in [g_par, g_sib, g_fwd, f_up, f_down, h_up, h_down, e_sib, e_par, *w_copies.values()]:
        copy.wait_send()
    for s in range(bits):
        for c in range(PARTS):
            stage(s, c).wait_send()


def shards(count, features, snake_alpha, down_weight, grad_out):
    frames, ci = features.shape
    units, pb = grad_out.shape
    width = TAPS * ci
    chunk = width // PARTS
    outs = 4 * pb
    rows = outs // count
    bits = count.bit_length() - 1
    half = outs // 2
    vm = pltpu.VMEM
    stages = [vm((PARTS, half >> s, chunk), BF) for s in range(bits)]
    sem = pltpu.SemaphoreType.DMA

    def body(*refs):
        ins, scratch = refs[:7], refs[7:]
        first, rest = scratch[:12], scratch[12:]
        sends, rest = rest[:bits], rest[bits:]
        recvs, rest = rest[:bits], rest[bits:]
        kernel(count, *ins, *first, sends, recvs, *rest)

    return pl.pallas_call(
        body,
        out_shape=(
            jax.ShapeDtypeStruct((units, pb), BF),
            jax.ShapeDtypeStruct((frames, ci), BF),
            jax.ShapeDtypeStruct((rows, TAPS, ci), BF),
        ),
        in_specs=[pl.BlockSpec(memory_space=vm)] * 4,
        out_specs=[pl.BlockSpec(memory_space=vm)] * 3,
        scratch_shapes=[
            vm((frames + 2 * HALO, ci), F32),
            vm((frames, ci), F32),
            vm((units, width), BF),
            vm((4, units, pb), BF),
            vm((outs, units), BF),
            vm((4, units, pb), BF),
            vm((4, units, pb), BF),
            vm((units + 2 * HALO, pb), F32),
            vm((width, 128), F32),
            vm((3, width, pb), BF),
            vm((4, width, pb), BF),
            vm((PARTS, half, chunk), F32),
            *stages,
            *stages,
            vm((4, units, pb), F32),
            vm((2, units, pb), BF),
            vm((2, units, pb), BF),
            vm((units, pb), BF),
            vm((units, pb), BF),
            vm((HALO, ci), BF),
            vm((HALO, ci), BF),
            vm((4, HALO, pb), BF),
            vm((4, HALO, pb), BF),
            vm((rows * TAPS, ci), F32),
            sem((2, 2)),
            sem((2, 3)),
            sem((2, 3)),
            sem((2, 2)),
            sem((2, bits * PARTS)),
            sem((2, 2)),
        ],
        compiler_params=pltpu.CompilerParams(
            collective_id=0, has_side_effects=True, vmem_limit_bytes=60 * 1024 * 1024
        ),
        cost_estimate=pl.CostEstimate(
            flops=6 * units * width * outs, bytes_accessed=4 * width * outs, transcendentals=0
        ),
        name="fused",
    )(features, snake_alpha.reshape(1, ci), down_weight, grad_out)


def solution(mesh):
    placed = (P("tm", "chan"), P("chan"), P(None, None, "chan"), P("tm", "chan"))
    return jax.shard_map(
        functools.partial(shards, mesh.shape["tm"]),
        mesh=mesh,
        in_specs=placed,
        out_specs=(P("tm", "chan"), P("tm", "chan"), P("tm", None, "chan")),
        check_vma=False,
    )
```

time: 405 us -> 94.7 us (0.23)
  waiting for transfers between devices: 279 us -> 0 us
  Pallas kernels: 0 us -> 88.6 us
  local copies, waits for them, and re-layouts: 46.2 us -> 5.27 us
  other arithmetic: 31.2 us -> 0 us
  matrix products: 23 us -> 0 us
  between operations: 14 us -> 0.64 us
  starting transfers between devices: 11.1 us -> 0 us
    reduce_scatter x2 -> x0, waiting for transfers between devices: 239 us -> none  [the longest x1 139 us: shards(): lax.psum_scatter(jnp.concatenate([lower, upper], axis=1), 'tm', scatter_d...]
    pallas_call x0 -> x1, Pallas kernels: none -> 88.6 us  [shards(): pl.pallas_call(body, out_shape=(jax.ShapeDtypeStruct((units, pb), BF), ja...]
    all_gather x2 -> x0, waiting for transfers between devices: 35.7 us -> none  [the longest x1 35.7 us: shards(): full_cols = lax.all_gather(padded, 'chan', axis=1, tiled=True)]
    convert_element_type x2 -> x0, other arithmetic: 24.4 us -> none  [the longest x1 23.1 us: shards(): (grad_snaked * (1.0 + jnp.sin(2.0 * snake_alpha * wide))).astype(jnp.bflo...]
    dot_general x6 -> x0, matrix products: 23 us -> none  [the longest x1 6.72 us: shards(): jnp.einsum('up,rjp->ujr', grad_pad[1:], down_weight[:, :STRIDE], preferre...]
    slice x5 -> x0, local copies, waits for them, and re-layouts: 19.4 us -> none  [the longest x1 10.9 us: shards(): spread.reshape(frames + STRIDE, down_weight.shape[0])]
    add x1 -> x0, local copies, waits for them, and re-layouts: 16.4 us -> none  [shards(): jnp.einsum('up,rjp->ujr', grad_pad[1:], down_weight[:, :STRIDE], preferre...]
    ppermute x4 -> x0, starting transfers between devices: 10.9 us -> none  [the longest x2 8.2 us: with_halo(): lax.ppermute(lax.slice_in_dim(block, block.shape[dim] - width, None, axis...]
  transfers between devices with their start and end apart: 8 -> 0, of which waited for: 4 -> 0; matrix products, arithmetic and copies ran while one was open for 16% -> 0% of each run, Pallas kernels for 0% -> 0%
where the time goes in v1:
time: 94.7 us; the launch traced here: 94.5 us
  Pallas kernels  88.6 us (94%)
  local copies, waits for them, and re-layouts  5.27 us (6%)
    pallas_call x1, Pallas kernels, shards(): pl.pallas_call(body, out_shape=(jax.ShapeDtypeStruct((units, pb), BF), ja...  88.6 us
    unnamed x5, local copies, waits for them, and re-layouts  5.27 us

profile of v1, /device:TPU:0, one launch (start us, length us, event | category | flops | bytes accessed | tf_op | source)
XLA Modules:
  0.0 94.5 jit_solution(8164411379385994359)
XLA Ops:
  0.6 88.6 %fused.1 = (bf16[768,256]{1,0:T(8,128)(2,1)}, bf16[6144,128]{1,0:T(8,128)(2,1)}, bf16[128,16,128]{2,1,0:T(8,128)(2,1)}) custom-call(bf16[6144,128]{1,0:T(8,128)(2,1)} %refs_0_.1, f32[1,128]{1,0:T(1,128)} %bitcast.1, bf16[512,16,256]{2,1,0:T(8,128)(2,1)} %refs_2_.1, bf16[768,256]{1,0:T(8,128)(2,1)} %refs_3_.1), custom_call_target="tpu_custom_call" | custom-call | flops 9663676416 | bytes 8388608 | tf_op jit(solution)/shard_map/fused/pallas_call | solution.py:327
  89.2 1.8 %copy.10 = bf16[768,256]{1,0:T(8,128)(2,1)} copy(bf16[768,256]{1,0:T(8,128)(2,1)} %get-tuple-element.6) | data formatting | bytes 786432
  91.0 0.0 copy-start
  91.0 2.7 %copy.11 = bf16[6144,128]{1,0:T(8,128)(2,1)} copy(bf16[6144,128]{1,0:T(8,128)(2,1)} %get-tuple-element.7) | data formatting | bytes 3145728
  93.7 0.0 copy-done
  93.7 0.8 copy.12
Async XLA Ops:
  91.0 2.7 %copy-start = (bf16[128,16,128]{2,1,0:T(8,128)(2,1)S(1)}, bf16[128,16,128]{2,1,0:T(8,128)(2,1)}, u32[]{:S(2)}) copy-start(bf16[128,16,128]{2,1,0:T(8,128)(2,1)} %get-tuple-element.8) | copy-start | bytes 1572868

commit v2 on v1

--- a/solution.py
+++ b/solution.py
@@ -11,7 +11,7 @@
 STRIDE = 8
 TAPS = 16
 HALO = 16
-PARTS = 4
+PARTS = 8
 BF = jnp.bfloat16
 F32 = jnp.float32
 
@@ -47,7 +47,7 @@
 def kernel(
     count, feat, alpha, weight, grad, enc_out, gf_out, gd_out,
     snaked, factor, cols, gfull, gturn, gprev, gnext, gwide,
-    wstage, wsend, wbuf, acc, sends, recvs, esum, esend, erecv, ysend, yrecv,
+    wstage, wsend, whalf, wbuf, acc, sends, recvs, esum, esend, erecv, ysend, yrecv,
     flow, fhigh, glow, ghigh, gdwide,
     fsem, gsem, wsem, hsem, rsem, esem,
 ):
@@ -69,7 +69,6 @@
     sib = flip(ch, 1)
     par = flip(ch, 2)
     opp = flip(sib, 2)
-    peers = (None, sib, par, opp)
 
     def remote(src, dst, sems, i, **where):
         return pltpu.make_async_remote_copy(
@@ -101,12 +100,27 @@
             for k in range(TAPS):
                 dst[pl.ds(k * ci, ci), lanes] = wstage[pl.ds(k, ci, stride=TAPS), :].astype(BF)
 
-    w_copies = {}
-    for r in (2, 3, 1):
-        turn(peers[r], wsend.at[r - 1])
-        w_copies[r] = remote(wsend.at[r - 1], wbuf.at[ch], wsem, r - 1, chan=peers[r])
-        w_copies[r].start()
-    turn(ch, wbuf.at[ch])
+    share = flip(t, 2)
+    hw = width // 2
+    htap = TAPS // 2
+    lot = lax.rem(t // 2, 2)
+
+    def turn_half(owner, their, dst):
+        for part in range(pb // 128):
+            lanes = pl.ds(part * 128, 128)
+            wstage[...] = weight[pl.ds(owner * ci, ci), :, lanes].astype(F32).reshape(ci * TAPS, 128)
+            for k in range(htap):
+                dst[pl.ds(k * ci, ci), lanes] = wstage[
+                    pl.ds(their * htap + k, ci, stride=TAPS), :
+                ].astype(BF)
+
+    got = pl.ds(pl.multiple_of(lot * hw, hw), hw)
+    w_par = remote(whalf.at[0], wbuf.at[ch, got], wsem, 1, chan=par)
+    w_opp = remote(whalf.at[1], wbuf.at[ch, got], wsem, 2, chan=opp)
+    w_par_on = remote(wbuf.at[par, got], wbuf.at[par, got], wsem, 3, tm=share)
+    w_opp_on = remote(wbuf.at[opp, got], wbuf.at[opp, got], wsem, 4, tm=share)
+    w_sib = remote(wsend, wbuf.at[ch], wsem, 0, chan=sib)
+    turn_half(par, lot, whalf.at[0])
     gfull[ch] = grad[...]
 
     a = alpha[...]
@@ -127,9 +141,6 @@
         return 0
 
     lax.fori_loop(0, frames // step, snake_step, 0)
-
-    g_par.wait_recv()
-    g_fwd.start()
 
     f_up.wait_recv()
     f_down.wait_recv()
@@ -142,24 +153,32 @@
             pl.ds(HALO - STRIDE // 2 + k, units, stride=STRIDE), :
         ].astype(BF)
 
+    def turn_grad(blk):
+        for part in range(pb // 128):
+            turned = gfull[blk, :, pl.ds(part * 128, 128)].astype(F32).T.astype(BF)
+            size = min(rows, 128)
+            for j in range(128 // size):
+                p = blk * pb + part * 128 + j * size
+                to = bit_reversed(p // rows, bits) * rows + p % rows
+                gturn[pl.ds(pl.multiple_of(to, size), size), :] = turned[
+                    j * size : (j + 1) * size, :
+                ]
+
+    turn_grad(ch)
     g_sib.wait_recv()
+    turn_grad(sib)
+    turn_half(opp, lot, whalf.at[1])
+    g_par.wait_recv()
+    g_fwd.start()
+    w_par.start()
+    w_opp.start()
+    turn_grad(par)
     g_fwd.wait_recv()
     h_up = remote(gfull.at[:, pl.ds(units - HALO, HALO), :], glow, hsem, 0, tm=nxt)
     h_down = remote(gfull.at[:, pl.ds(0, HALO), :], ghigh, hsem, 1, tm=prv)
     h_up.start()
     h_down.start()
-
-    for blk in range(4):
-        for part in range(pb // 128):
-            turned = gfull[blk, :, pl.ds(part * 128, 128)].astype(F32).T.astype(BF)
-            first = blk * pb + part * 128
-            size = min(rows, 128)
-            for j in range(128 // size):
-                p = first + j * size
-                d, rest = p // rows, p % rows
-                gturn[pl.ds(bit_reversed(d, bits) * rows + rest, size), :] = turned[
-                    j * size : (j + 1) * size, :
-                ]
+    turn_grad(opp)
 
     bit_of = [lax.rem(t // (1 << s), 2) for s in range(bits)]
     half = outs // 2
@@ -185,6 +204,9 @@
         return 0
 
     lax.fori_loop(0, PARTS, second_half, 0)
+    turn(sib, wsend)
+    w_sib.start()
+    turn(ch, wbuf.at[ch])
 
     scale = 1.0 / math.sqrt(units * count)
 
@@ -217,15 +239,17 @@
                 gdwide[pl.ds(c * taps + j, size, stride=TAPS), :] = total[:, j * ci : (j + 1) * ci]
 
     events = sorted(
-        ((c + s * 1.3, s, c) for s in range(bits) for c in range(PARTS))
+        ((c + s * 0.9, s, c) for s in range(bits) for c in range(PARTS))
     )
     events = [(s, c) for _, s, c in events]
 
     def run(limit):
-        while events and events[0][1] + events[0][0] <= limit:
+        while events and events[0][1] + events[0][0] * 0.9 <= limit:
             advance(*events.pop(0))
 
-    run(2)
+    w_par.wait_recv()
+    w_par_on.start()
+    run(1)
 
     h_up.wait_recv()
     h_down.wait_recv()
@@ -240,8 +264,12 @@
 
     lax.fori_loop(0, 4, shifted, 0)
 
-    for r in (1, 2, 3):
-        w_copies[r].wait_recv()
+    w_opp.wait_recv()
+    w_opp_on.start()
+    run(3.5)
+    w_sib.wait_recv()
+    w_par_on.wait_recv()
+    w_opp_on.wait_recv()
 
     def encode(d, _):
         esum[d] = dot(cols[...], wbuf[d], ((1,), (0,)))
@@ -254,7 +282,7 @@
     e_par = remote(ysend, yrecv, esem, 1, chan=par)
     e_sib.start()
 
-    run(3)
+    run(4)
 
     e_sib.wait_recv()
     ysend[...] = (esum[par] + erecv[1].astype(F32)).astype(BF)
@@ -263,8 +291,10 @@
     quarter = 4 * ci
     tile = units // 3
 
-    def spread(i, _):
-        at = pl.multiple_of(i * tile, tile)
+    run(4.5)
+
+    def spread(i):
+        at = i * tile
         us = pl.ds(at, tile)
         for lo, own, side, shift in ((0, 1, 3, gprev), (4, 2, 0, gnext)):
             total = jnp.zeros((tile, quarter), F32)
@@ -279,9 +309,13 @@
                 snaked[pl.ds(at * STRIDE + lo + j, tile, stride=STRIDE), :] = total[
                     :, j * ci : (j + 1) * ci
                 ]
-        return 0
-
-    lax.fori_loop(0, 3, spread, 0)
+
+    spread(0)
+    run(5)
+    spread(1)
+    run(5.5)
+    spread(2)
+    run(6)
 
     def finish(i, _):
         at = pl.multiple_of(i * step, step)
@@ -297,7 +331,8 @@
     run(100)
     gd_out[...] = gdwide[...].reshape(rows, TAPS, ci).astype(BF)
 
-    for copy in [g_par, g_sib, g_fwd, f_up, f_down, h_up, h_down, e_sib, e_par, *w_copies.values()]:
+    started = [g_par, g_sib, g_fwd, f_up, f_down, h_up, h_down, e_sib, e_par]
+    for copy in started + [w_sib, w_par, w_opp, w_par_on, w_opp_on]:
         copy.wait_send()
     for s in range(bits):
         for c in range(PARTS):
@@ -319,7 +354,7 @@
 
     def body(*refs):
         ins, scratch = refs[:7], refs[7:]
-        first, rest = scratch[:12], scratch[12:]
+        first, rest = scratch[:13], scratch[13:]
         sends, rest = rest[:bits], rest[bits:]
         recvs, rest = rest[:bits], rest[bits:]
         kernel(count, *ins, *first, sends, recvs, *rest)
@@ -343,7 +378,8 @@
             vm((4, units, pb), BF),
             vm((units + 2 * HALO, pb), F32),
             vm((width, 128), F32),
-            vm((3, width, pb), BF),
+            vm((width, pb), BF),
+            vm((2, width // 2, pb), BF),
             vm((4, width, pb), BF),
             vm((PARTS, half, chunk), F32),
             *stages,
@@ -360,7 +396,7 @@
             vm((rows * TAPS, ci), F32),
             sem((2, 2)),
             sem((2, 3)),
-            sem((2, 3)),
+            sem((2, 5)),
             sem((2, 2)),
             sem((2, bits * PARTS)),
             sem((2, 2)),

time: 94.7 us -> 106 us (1.12)
  Pallas kernels: 88.6 us -> 100 us
    pallas_call x1, Pallas kernels: 88.6 us -> 100 us  [shards(): pl.pallas_call(body, out_shape=(jax.ShapeDtypeStruct((units, pb), BF), ja...]
where the time goes in v2:
time: 106 us
  Pallas kernels  100 us (94%)
  local copies, waits for them, and re-layouts  5.27 us (5%)
    pallas_call x1, Pallas kernels, shards(): pl.pallas_call(body, out_shape=(jax.ShapeDtypeStruct((units, pb), BF), ja...  100 us
    unnamed x5, local copies, waits for them, and re-layouts  5.27 us

profile of v2, /device:TPU:0, one launch (start us, length us, event | category | flops | bytes accessed | tf_op | source)
XLA Modules:
  0.0 106.1 jit_solution(3183696729397255308)
XLA Ops:
  0.6 100.2 %fused.1 = (bf16[768,256]{1,0:T(8,128)(2,1)}, bf16[6144,128]{1,0:T(8,128)(2,1)}, bf16[128,16,128]{2,1,0:T(8,128)(2,1)}) custom-call(bf16[6144,128]{1,0:T(8,128)(2,1)} %refs_0_.1, f32[1,128]{1,0:T(1,128)} %bitcast.1, bf16[512,16,256]{2,1,0:T(8,128)(2,1)} %refs_2_.1, bf16[768,256]{1,0:T(8,128)(2,1)} %refs_3_.1), custom_call_target="tpu_custom_call" | custom-call | flops 9663676416 | bytes 8388608 | tf_op jit(solution)/shard_map/fused/pallas_call | solution.py:362
  100.9 1.8 %copy.10 = bf16[768,256]{1,0:T(8,128)(2,1)} copy(bf16[768,256]{1,0:T(8,128)(2,1)} %get-tuple-element.6) | data formatting | bytes 786432
  102.6 0.0 copy-start
  102.6 2.7 %copy.11 = bf16[6144,128]{1,0:T(8,128)(2,1)} copy(bf16[6144,128]{1,0:T(8,128)(2,1)} %get-tuple-element.7) | data formatting | bytes 3145728
  105.4 0.0 copy-done
  105.4 0.8 copy.12
Async XLA Ops:
  102.6 2.7 %copy-start = (bf16[128,16,128]{2,1,0:T(8,128)(2,1)S(1)}, bf16[128,16,128]{2,1,0:T(8,128)(2,1)}, u32[]{:S(2)}) copy-start(bf16[128,16,128]{2,1,0:T(8,128)(2,1)} %get-tuple-element.8) | copy-start | bytes 1572868

commit v3 on v2

--- a/solution.py
+++ b/solution.py
@@ -12,6 +12,7 @@
 TAPS = 16
 HALO = 16
 PARTS = 8
+AHEAD = 2
 BF = jnp.bfloat16
 F32 = jnp.float32
 
@@ -121,6 +122,11 @@
     w_opp_on = remote(wbuf.at[opp, got], wbuf.at[opp, got], wsem, 4, tm=share)
     w_sib = remote(wsend, wbuf.at[ch], wsem, 0, chan=sib)
     turn_half(par, lot, whalf.at[0])
+    w_par.start()
+    turn_half(opp, lot, whalf.at[1])
+    w_opp.start()
+    turn(sib, wsend)
+    w_sib.start()
     gfull[ch] = grad[...]
 
     a = alpha[...]
@@ -167,11 +173,8 @@
     turn_grad(ch)
     g_sib.wait_recv()
     turn_grad(sib)
-    turn_half(opp, lot, whalf.at[1])
     g_par.wait_recv()
     g_fwd.start()
-    w_par.start()
-    w_opp.start()
     turn_grad(par)
     g_fwd.wait_recv()
     h_up = remote(gfull.at[:, pl.ds(units - HALO, HALO), :], glow, hsem, 0, tm=nxt)
@@ -193,10 +196,14 @@
     def first_half(c, _):
         lanes = pl.ds(pl.multiple_of(c * chunk, chunk), chunk)
         sends[0][c] = dot(gturn[pl.ds(other, half), :], cols[:, lanes], ((1,), (0,))).astype(BF)
+        return 0
+
+    for c in range(AHEAD):
+        first_half(c, 0)
         stage(0, c).start()
-        return 0
-
-    lax.fori_loop(0, PARTS, first_half, 0)
+    w_par.wait_recv()
+    w_par_on.start()
+    lax.fori_loop(AHEAD, PARTS, first_half, 0)
 
     def second_half(c, _):
         lanes = pl.ds(pl.multiple_of(c * chunk, chunk), chunk)
@@ -204,8 +211,6 @@
         return 0
 
     lax.fori_loop(0, PARTS, second_half, 0)
-    turn(sib, wsend)
-    w_sib.start()
     turn(ch, wbuf.at[ch])
 
     scale = 1.0 / math.sqrt(units * count)
@@ -218,6 +223,8 @@
         size = half >> s
         copy = stage(s, c)
         copy.wait_recv()
+        if s == 0 and c + AHEAD < PARTS:
+            stage(0, c + AHEAD).start()
         if s + 1 < bits:
             nsize = size // 2
             keep = pl.multiple_of(base[s + 1], nsize)
@@ -247,9 +254,7 @@
         while events and events[0][1] + events[0][0] * 0.9 <= limit:
             advance(*events.pop(0))
 
-    w_par.wait_recv()
-    w_par_on.start()
-    run(1)
+    run(0)
 
     h_up.wait_recv()
     h_down.wait_recv()
@@ -266,7 +271,7 @@
 
     w_opp.wait_recv()
     w_opp_on.start()
-    run(3.5)
+    run(3)
     w_sib.wait_recv()
     w_par_on.wait_recv()
     w_opp_on.wait_recv()

time: 106 us -> 108 us (1.019)
  Pallas kernels: 100 us -> 102 us
    pallas_call x1, Pallas kernels: 100 us -> 102 us  [shards(): pl.pallas_call(body, out_shape=(jax.ShapeDtypeStruct((units, pb), BF), ja...]
where the time goes in v3:
time: 108 us
  Pallas kernels  102 us (94%)
  local copies, waits for them, and re-layouts  5.27 us (5%)
    pallas_call x1, Pallas kernels, shards(): pl.pallas_call(body, out_shape=(jax.ShapeDtypeStruct((units, pb), BF), ja...  102 us
    unnamed x5, local copies, waits for them, and re-layouts  5.27 us

profile of v3, /device:TPU:0, one launch (start us, length us, event | category | flops | bytes accessed | tf_op | source)
XLA Modules:
  0.0 107.9 jit_solution(14208144314558103264)
XLA Ops:
  0.6 102.0 %fused.1 = (bf16[768,256]{1,0:T(8,128)(2,1)}, bf16[6144,128]{1,0:T(8,128)(2,1)}, bf16[128,16,128]{2,1,0:T(8,128)(2,1)}) custom-call(bf16[6144,128]{1,0:T(8,128)(2,1)} %refs_0_.1, f32[1,128]{1,0:T(1,128)} %bitcast.1, bf16[512,16,256]{2,1,0:T(8,128)(2,1)} %refs_2_.1, bf16[768,256]{1,0:T(8,128)(2,1)} %refs_3_.1), custom_call_target="tpu_custom_call" | custom-call | flops 9663676416 | bytes 8388608 | tf_op jit(solution)/shard_map/fused/pallas_call | solution.py:367
  102.7 1.8 %copy.10 = bf16[768,256]{1,0:T(8,128)(2,1)} copy(bf16[768,256]{1,0:T(8,128)(2,1)} %get-tuple-element.6) | data formatting | bytes 786432
  104.4 0.0 copy-start
  104.4 2.7 %copy.11 = bf16[6144,128]{1,0:T(8,128)(2,1)} copy(bf16[6144,128]{1,0:T(8,128)(2,1)} %get-tuple-element.7) | data formatting | bytes 3145728
  107.1 0.0 copy-done
  107.1 0.8 copy.12
Async XLA Ops:
  104.4 2.7 %copy-start = (bf16[128,16,128]{2,1,0:T(8,128)(2,1)S(1)}, bf16[128,16,128]{2,1,0:T(8,128)(2,1)}, u32[]{:S(2)}) copy-start(bf16[128,16,128]{2,1,0:T(8,128)(2,1)} %get-tuple-element.8) | copy-start | bytes 1572868

commit v4 on v1

--- a/solution.py
+++ b/solution.py
@@ -11,7 +11,7 @@
 STRIDE = 8
 TAPS = 16
 HALO = 16
-PARTS = 4
+PARTS = 8
 BF = jnp.bfloat16
 F32 = jnp.float32
 
@@ -106,7 +106,6 @@
         turn(peers[r], wsend.at[r - 1])
         w_copies[r] = remote(wsend.at[r - 1], wbuf.at[ch], wsem, r - 1, chan=peers[r])
         w_copies[r].start()
-    turn(ch, wbuf.at[ch])
     gfull[ch] = grad[...]
 
     a = alpha[...]
@@ -185,6 +184,7 @@
         return 0
 
     lax.fori_loop(0, PARTS, second_half, 0)
+    turn(ch, wbuf.at[ch])
 
     scale = 1.0 / math.sqrt(units * count)
 
@@ -217,12 +217,12 @@
                 gdwide[pl.ds(c * taps + j, size, stride=TAPS), :] = total[:, j * ci : (j + 1) * ci]
 
     events = sorted(
-        ((c + s * 1.3, s, c) for s in range(bits) for c in range(PARTS))
+        ((c + s * 0.9, s, c) for s in range(bits) for c in range(PARTS))
     )
     events = [(s, c) for _, s, c in events]
 
     def run(limit):
-        while events and events[0][1] + events[0][0] <= limit:
+        while events and events[0][1] + events[0][0] * 0.9 <= limit:
             advance(*events.pop(0))
 
     run(2)
@@ -240,6 +240,7 @@
 
     lax.fori_loop(0, 4, shifted, 0)
 
+    run(5)
     for r in (1, 2, 3):
         w_copies[r].wait_recv()
 
@@ -254,7 +255,7 @@
     e_par = remote(ysend, yrecv, esem, 1, chan=par)
     e_sib.start()
 
-    run(3)
+    run(5.9)
 
     e_sib.wait_recv()
     ysend[...] = (esum[par] + erecv[1].astype(F32)).astype(BF)
@@ -263,8 +264,8 @@
     quarter = 4 * ci
     tile = units // 3
 
-    def spread(i, _):
-        at = pl.multiple_of(i * tile, tile)
+    def spread(i):
+        at = i * tile
         us = pl.ds(at, tile)
         for lo, own, side, shift in ((0, 1, 3, gprev), (4, 2, 0, gnext)):
             total = jnp.zeros((tile, quarter), F32)
@@ -279,9 +280,13 @@
                 snaked[pl.ds(at * STRIDE + lo + j, tile, stride=STRIDE), :] = total[
                     :, j * ci : (j + 1) * ci
                 ]
-        return 0
-
-    lax.fori_loop(0, 3, spread, 0)
+
+    spread(0)
+    run(6.9)
+    spread(1)
+    run(7.9)
+    spread(2)
+    run(8)
 
     def finish(i, _):
         at = pl.multiple_of(i * step, step)

time: 94.7 us -> 93 us (0.982)
  Pallas kernels: 88.6 us -> 86.9 us
    pallas_call x1, Pallas kernels: 88.6 us -> 86.9 us  [shards(): pl.pallas_call(body, out_shape=(jax.ShapeDtypeStruct((units, pb), BF), ja...]
where the time goes in v4:
time: 93 us; the launch traced here: 92.9 us
  Pallas kernels  86.9 us (93%)
  local copies, waits for them, and re-layouts  5.27 us (6%)
    pallas_call x1, Pallas kernels, shards(): pl.pallas_call(body, out_shape=(jax.ShapeDtypeStruct((units, pb), BF), ja...  86.9 us
    unnamed x5, local copies, waits for them, and re-layouts  5.27 us

profile of v4, /device:TPU:0, one launch (start us, length us, event | category | flops | bytes accessed | tf_op | source)
XLA Modules:
  0.0 92.9 jit_solution(3078546902574310604)
XLA Ops:
  0.6 86.9 %fused.1 = (bf16[768,256]{1,0:T(8,128)(2,1)}, bf16[6144,128]{1,0:T(8,128)(2,1)}, bf16[128,16,128]{2,1,0:T(8,128)(2,1)}) custom-call(bf16[6144,128]{1,0:T(8,128)(2,1)} %refs_0_.1, f32[1,128]{1,0:T(1,128)} %bitcast.1, bf16[512,16,256]{2,1,0:T(8,128)(2,1)} %refs_2_.1, bf16[768,256]{1,0:T(8,128)(2,1)} %refs_3_.1), custom_call_target="tpu_custom_call" | custom-call | flops 9663676416 | bytes 8388608 | tf_op jit(solution)/shard_map/fused/pallas_call | solution.py:332
  87.6 1.8 %copy.10 = bf16[768,256]{1,0:T(8,128)(2,1)} copy(bf16[768,256]{1,0:T(8,128)(2,1)} %get-tuple-element.6) | data formatting | bytes 786432
  89.4 0.0 copy-start
  89.4 2.7 %copy.11 = bf16[6144,128]{1,0:T(8,128)(2,1)} copy(bf16[6144,128]{1,0:T(8,128)(2,1)} %get-tuple-element.7) | data formatting | bytes 3145728
  92.1 0.0 copy-done
  92.1 0.8 copy.12
Async XLA Ops:
  89.4 2.7 %copy-start = (bf16[128,16,128]{2,1,0:T(8,128)(2,1)S(1)}, bf16[128,16,128]{2,1,0:T(8,128)(2,1)}, u32[]{:S(2)}) copy-start(bf16[128,16,128]{2,1,0:T(8,128)(2,1)} %get-tuple-element.8) | copy-start | bytes 1572868
